TPU v7x, 32 devices: a whole 2x2x4 slice. The times are simulated.
32 devices in a mesh: ctx: 8 (over y, x, core), kvh: 4 (over z).
Axes of the slice: x: 2, y: 2, z: 4, core: 2. Of those that a mesh axis runs over, the one named last changes fastest.
Arguments:
- x_kv: bfloat16 [2048, 3072], P('ctx'), may hold values from -17 to 17, as said below
- w_kv: bfloat16 [3072, 2048], P(None, 'kvh'), may hold values from -0.0546875 to 0.0546875
- queries: bfloat16 [3, 3072, 3072], P(None, 'ctx', 'kvh'), may hold values from -6 to 6
- d_out: bfloat16 [3, 3072, 3072], P(None, 'ctx', 'kvh'), may hold values from -12 to 12
- lse: float32 [3, 3072, 24], P(None, 'ctx', 'kvh'), may hold values from 7 to 10
- delta: float32 [3, 3072, 24], P(None, 'ctx', 'kvh'), may hold values from -24 to 24
- offsets: int32 [8], P('ctx'), may hold values from 1 to 2047
- block_mask: int32 [24, 16], P('ctx'), may hold values 0 or 1
Outputs:
- d_queries: bfloat16 [3, 3072, 3072], P(None, 'ctx', 'kvh')
- d_x: bfloat16 [2048, 3072], P('ctx', 'kvh')
- d_w: float32 [3072, 2048], P('ctx', 'kvh')
Inputs may be any that keep to these rules, and one draw needn't show every extreme that they name: `x_kv`: feature scales differ from column to column.
All inputs are finite; a program needn't handle non-finite values.
Results may differ from a plain program's by a relative error of at most 0.012.
Values may be sent and summed in bfloat16 or wider, within the bound.
A program may use at most 64 MiB of HBM per device.

v0:
```python
import jax
import jax.numpy as jnp
from jax import lax
from jax.sharding import PartitionSpec as P

D = 3072
KVH = 8
HD = 128
QBLK = 128
KBLK = 128


key_span = 512


def body(x_kv, w_kv, queries, d_out, lse, delta, offsets, block_mask):
    layers, qrows, width = queries.shape
    kvd = w_kv.shape[1] // (2 * HD)
    groups = width // (HD * kvd)
    columns = kvd * 2 * HD
    scale = HD ** (-0.5)
    kv_local = jnp.dot(x_kv, w_kv, preferred_element_type=jnp.float32).astype(jnp.bfloat16)
    own_keys = kv_local.shape[0]
    total_keys = own_keys * lax.axis_size("ctx")
    qblocks, kblocks = block_mask.shape
    allowed = jnp.broadcast_to(
        (block_mask == 1)[:, None, :, None], (qblocks, QBLK, kblocks, KBLK)
    ).reshape(qrows, total_keys)
    limit = offsets[0] + jnp.arange(qrows, dtype=jnp.int32)
    q_split = queries.reshape(layers, qrows, kvd, groups, HD)
    output_split = d_out.reshape(layers, qrows, kvd, groups, HD)
    lse_t = jnp.transpose(lse.reshape(layers, qrows, kvd, groups), (0, 2, 3, 1))[..., None]
    delta_t = jnp.transpose(delta.reshape(layers, qrows, kvd, groups), (0, 2, 3, 1))[..., None]

    def block_terms(kblock, kstart):
        count = kblock.shape[0]
        key_value_four = kblock.reshape(count, kvd, 2, HD)
        kmat = key_value_four[:, :, 0, :]
        value_matrix = key_value_four[:, :, 1, :]
        positions = kstart + jnp.arange(count, dtype=jnp.int32)
        visible = lax.dynamic_slice_in_dim(allowed, kstart, count, 1) & (
            positions[None, :] < limit[:, None]
        )
        dq_terms = []
        dkv_total = jnp.zeros((count, columns), jnp.float32)
        for layer_index in range(layers):
            scores = (
                jnp.einsum(
                    "uyeb,pyb->yeup", q_split[layer_index], kmat, preferred_element_type=jnp.float32
                )
                * scale
            )
            probs = jnp.where(visible, jnp.exp(scores - lse_t[layer_index]), jnp.float32(0.0))
            probability_gradient = jnp.einsum(
                "uyeb,pyb->yeup",
                output_split[layer_index],
                value_matrix,
                preferred_element_type=jnp.float32,
            )
            dscore = (probs * (probability_gradient - delta_t[layer_index])).astype(jnp.bfloat16)
            dq_part = (
                jnp.einsum("kgqn,nkd->qkgd", dscore, kmat, preferred_element_type=jnp.float32)
                * scale
            )
            dq_terms.append(dq_part)
            p_half = probs.astype(jnp.bfloat16)
            dv_part = jnp.einsum(
                "kgqn,qkgd->nkd",
                p_half,
                output_split[layer_index],
                preferred_element_type=jnp.float32,
            )
            dk_part = (
                jnp.einsum(
                    "kgqn,qkgd->nkd",
                    dscore,
                    q_split[layer_index],
                    preferred_element_type=jnp.float32,
                )
                * scale
            )
            dkv_total = dkv_total + jnp.stack([dk_part, dv_part], axis=2).reshape(count, columns)
        dq_stack = jnp.stack(dq_terms, axis=0)
        return (dq_stack, dkv_total)

    dq_init = jnp.zeros((layers, qrows, kvd, groups, HD), jnp.float32)
    second_init = jnp.zeros((total_keys, columns), jnp.float32)
    kv_whole = lax.all_gather(kv_local, "ctx", axis=0, tiled=True)
    count = kv_whole.shape[0]

    def one_block(inner, kblock, at):
        dq_acc, second = inner
        dq_part, dkv_part = block_terms(kblock, at)
        current = lax.dynamic_slice_in_dim(second, at, kblock.shape[0], 0)
        return (
            dq_acc + dq_part,
            lax.dynamic_update_slice_in_dim(second, current + dkv_part, at, 0),
        )

    def step_block(index, inner):
        offset = index * key_span
        kblock = lax.dynamic_slice_in_dim(kv_whole, offset, key_span, 0)
        return one_block(inner, kblock, offset)

    dq_acc, second_acc = lax.fori_loop(0, count // key_span, step_block, (dq_init, second_init))
    dkv_own = lax.psum_scatter(second_acc, "ctx", scatter_dimension=0, tiled=True)
    dkv_half = dkv_own.astype(jnp.bfloat16)
    dx_part = lax.dot_general(
        dkv_half, w_kv, (((1,), (1,)), ((), ())), preferred_element_type=jnp.float32
    )
    dw_part = lax.dot_general(
        x_kv, dkv_half, (((0,), (0,)), ((), ())), preferred_element_type=jnp.float32
    )
    d_x = lax.psum_scatter(dx_part, "kvh", scatter_dimension=1, tiled=True).astype(jnp.bfloat16)
    grad = lax.psum_scatter(dw_part, "ctx", scatter_dimension=0, tiled=True)
    squares = lax.psum(jnp.sum(grad * grad), ("ctx", "kvh"))
    d_w = grad / jnp.sqrt(squares / (D * KVH * 2 * HD) + 1e-06)
    d_queries = dq_acc.reshape(layers, qrows, width).astype(jnp.bfloat16)
    return (d_queries, d_x, d_w)


def solution(mesh):
    in_specs = (
        P("ctx", None),
        P(None, "kvh"),
        P(None, "ctx", "kvh"),
        P(None, "ctx", "kvh"),
        P(None, "ctx", "kvh"),
        P(None, "ctx", "kvh"),
        P("ctx"),
        P("ctx", None),
    )
    out_specs = (P(None, "ctx", "kvh"), P("ctx", "kvh"), P("ctx", "kvh"))
    return jax.shard_map(body, mesh=mesh, in_specs=in_specs, out_specs=out_specs, check_vma=False)
```

profile of v0, /device:TPU:0, one launch (start us, length us, event | category | flops | bytes accessed | tf_op | source)
XLA Modules:
  0.0 405.5 jit_solution(15823705586697455860)
XLA Ops:
  7.3 1.8 copy-done
  9.1 3.1 convolution_convert_fusion
  14.0 3.8 copy.53
  17.8 3.8 copy.59
  21.6 3.9 copy.55
  25.5 3.9 copy.61
  29.3 13.6 %all-gather.2.cloned.1.call-done = bf16[2048,512]{1,0:T(8,128)(2,1)} async-done(((bf16[256,512]{1,0:T(8,128)(2,1)}), bf16[2048,512]{1,0:T(8,128)(2,1)}) %all-gather.2.cloned.1.call-update) | async-done | bytes 2097168 | tf_op jit(solution)/shard_map/all_gather | solution.py:88
  42.9 2.5 broadcast_in_dim.45
  45.4 125.0 %while.16 = (s32[]{:T(128)}, f32[3,384,2,3,128]{1,4,3,2,0:T(8,128)}, f32[2048,512]{0,1:T(8,128)}, bf16[2048,512]{1,0:T(8,128)(2,1)}, pred[384,2048]{1,0:T(8,128)...) while((s32[]{:T(128)}, ...), condition=%wide.region_1.2_spmd.clone, body=%wide.region_0.1_spmd.clone.sunk | while | flops 4572021760 | bytes 149753440 | solution.py:105
  49.5 1.9 constant_dynamic-slice_fusion.4
  51.4 2.0 copy.107
  53.4 2.1 fusion.155
  56.8 1.7 fusion.156
  62.0 1.8 fusion.153
  67.3 1.8 fusion.150
  73.4 3.2 constant_dynamic-update-slice_fusion.2
  80.7 1.9 constant_dynamic-slice_fusion.4
  82.5 2.0 copy.107
  84.6 2.1 fusion.155
  87.9 1.7 fusion.156
  93.2 1.8 fusion.153
  98.5 1.8 fusion.150
  104.5 3.2 constant_dynamic-update-slice_fusion.2
  111.8 1.9 constant_dynamic-slice_fusion.4
  113.7 2.0 copy.107
  115.8 2.1 fusion.155
  119.1 1.7 fusion.156
  124.4 1.8 fusion.153
  129.7 1.8 fusion.150
  135.7 3.2 constant_dynamic-update-slice_fusion.2
  143.0 1.9 constant_dynamic-slice_fusion.4
  144.9 2.0 copy.107
  147.0 2.1 fusion.155
  155.6 1.8 fusion.153
  160.9 1.8 fusion.150
  166.9 3.3 constant_dynamic-update-slice_fusion.2
  170.5 51.5 %reduce-scatter.4.cloned.1.call-done = f32[256,512]{0,1:T(8,128)} async-done(((f32[2048,512]{0,1:T(8,128)}), f32[256,512]{0,1:T(8,128)}) %reduce-scatter.4.cloned.1.call-update) | async-done | bytes 524304 | tf_op jit(solution)/shard_map/reduce_scatter | solution.py:106
  221.9 5.2 %convolution_bitcast_fusion.3 = f32[3072,512]{0,1:T(8,128)} fusion(bf16[256,3072]{1,0:T(8,128)(2,1)} %param.10, f32[256,512]{0,1:T(8,128)} %reduce-scatter.4.cloned.1.call-done), kind=kOutput, calls=%fused_computation.97 | convolution fusion | flops 805437440 | bytes 8388608 | tf_op jit(solution)/shard_map/dot_general | solution.py:111
  227.2 3.8 fusion.79
  231.0 3.8 convert_element_type.58
  234.9 4.0 copy.63
  238.9 50.2 %reduce-scatter.8.cloned.1.call-done = f32[384,512]{0,1:T(8,128)} async-done(((f32[3072,512]{0,1:T(8,128)}), f32[384,512]{0,1:T(8,128)}) %reduce-scatter.8.cloned.1.call-update) | async-done | bytes 786448 | tf_op jit(solution)/shard_map/reduce_scatter | solution.py:115
  289.1 1.9 multiply_reduce_fusion
  291.0 60.5 %reduce-scatter.6.cloned.1.call-done = f32[256,768]{1,0:T(8,128)} async-done(((f32[256,3072]{1,0:T(8,128)}), f32[256,768]{1,0:T(8,128)}) %reduce-scatter.6.cloned.1.call-update) | async-done | bytes 786448 | tf_op jit(solution)/shard_map/reduce_scatter | solution.py:114
  351.5 1.9 convert_element_type.61
  353.4 40.4 %psum.7 = f32[]{:T(128)} all-reduce(f32[]{:T(128)} %multiply_reduce_fusion), channel_id=1, replica_groups=mesh['ctx'=8,'kvh'=4] {'ctx','kvh'}, use_global_device_ids=true, to_apply=%region_6.7 | all-reduce | flops 1 | bytes 8 | tf_op jit(solution)/shard_map/psum | solution.py:116
  394.5 2.1 broadcast_divide_fusion
  396.6 2.3 copy.64
  (216 shorter events, 69.2 us)
Async XLA Ops:
  7.2 1.9 copy-start
  7.2 5.1 %copy-start.15 = (f32[3,384,6]{1,2,0:T(8,128)S(1)}, f32[3,384,6]{1,2,0:T(8,128)}, u32[]{:S(2)}) copy-start(f32[3,384,6]{1,2,0:T(8,128)} %param.14) | copy-start | bytes 82948
  7.2 5.1 %copy-start.16 = (f32[3,384,6]{1,2,0:T(8,128)S(1)}, f32[3,384,6]{1,2,0:T(8,128)}, u32[]{:S(2)}) copy-start(f32[3,384,6]{1,2,0:T(8,128)} %param.15) | copy-start | bytes 82948
  7.2 5.1 %copy-start.17 = (s32[3,16]{1,0:T(4,128)S(1)}, s32[3,16]{1,0:T(4,128)}, u32[]{:S(2)}) copy-start(s32[3,16]{1,0:T(4,128)} %param.17) | copy-start | bytes 580
  7.2 35.7 %all-gather.2.cloned.1.call-start = ((), (), s32[]{:S(2)}) async-start(), calls=%async_computation.3 | async-start | bytes 2359296 | tf_op jit(solution)/shard_map/all_gather | solution.py:88
  12.2 209.7 %reduce-scatter.4.cloned.1.call-start = ((), (), s32[]{:S(2)}) async-start(), calls=%async_computation.4 | async-start | bytes 4718592 | tf_op jit(solution)/shard_map/reduce_scatter | solution.py:106
  45.4 1.9 copy-start.6
  45.4 1.9 copy-start.8
  51.4 4.2 %copy-start.14 = (f32[2,3,384]{2,1,0:T(4,128)S(1)}, f32[2,3,384]{2,1,0:T(4,128)}, u32[]{:S(2)}) copy-start(f32[2,3,384]{2,1,0:T(4,128)} %get-tuple-element.328) | copy-start | bytes 27652 | tf_op jit(solution)/shard_map/while
  53.4 2.1 copy-start.5
  55.5 1.2 copy-start.2
  55.5 1.2 copy-start.13
  56.7 1.7 copy-start.1
  70.0 2.0 copy-start.3
  73.2 3.3 copy-start.4
  73.3 3.3 copy-start.7
  73.3 3.3 copy-start.9
  76.6 1.9 copy-start.6
  76.6 1.9 copy-start.8
  82.5 4.2 %copy-start.14 = (f32[2,3,384]{2,1,0:T(4,128)S(1)}, f32[2,3,384]{2,1,0:T(4,128)}, u32[]{:S(2)}) copy-start(f32[2,3,384]{2,1,0:T(4,128)} %get-tuple-element.328) | copy-start | bytes 27652 | tf_op jit(solution)/shard_map/while
  84.6 2.1 copy-start.5
  86.7 1.2 copy-start.2
  86.7 1.2 copy-start.13
  87.9 1.7 copy-start.1
  101.2 2.0 copy-start.3
  104.4 3.3 copy-start.4
  104.4 3.3 copy-start.7
  104.4 3.3 copy-start.9
  107.7 1.9 copy-start.6
  107.7 1.9 copy-start.8
  113.7 4.2 %copy-start.14 = (f32[2,3,384]{2,1,0:T(4,128)S(1)}, f32[2,3,384]{2,1,0:T(4,128)}, u32[]{:S(2)}) copy-start(f32[2,3,384]{2,1,0:T(4,128)} %get-tuple-element.328) | copy-start | bytes 27652 | tf_op jit(solution)/shard_map/while
  115.8 2.1 copy-start.5
  119.1 1.7 copy-start.1
  132.4 2.0 copy-start.3
  135.6 3.3 copy-start.4
  135.6 3.3 copy-start.7
  135.6 3.3 copy-start.9
  138.9 1.9 copy-start.6
  138.9 1.9 copy-start.8
  144.9 4.2 %copy-start.14 = (f32[2,3,384]{2,1,0:T(4,128)S(1)}, f32[2,3,384]{2,1,0:T(4,128)}, u32[]{:S(2)}) copy-start(f32[2,3,384]{2,1,0:T(4,128)} %get-tuple-element.328) | copy-start | bytes 27652 | tf_op jit(solution)/shard_map/while
  147.0 2.1 copy-start.5
  150.3 1.7 copy-start.1
  163.6 2.0 copy-start.3
  166.8 3.4 copy-start.4
  166.8 3.4 copy-start.7
  166.8 3.4 copy-start.9
  170.4 118.6 %reduce-scatter.8.cloned.1.call-start = ((), (), s32[]{:S(2)}) async-start(), calls=%async_computation.6 | async-start | bytes 7077888 | tf_op jit(solution)/shard_map/reduce_scatter | solution.py:115
  227.2 124.3 %reduce-scatter.6.cloned.1.call-start = ((), (), s32[]{:S(2)}) async-start(), calls=%async_computation.5 | async-start | bytes 3932160 | tf_op jit(solution)/shard_map/reduce_scatter | solution.py:114
  (16 other events, 16.2 us)
Sparse Core Ops, SparseCore 0:
  12.3 30.5 all-gather.1
  170.5 51.3 reduce-scatter.3
  227.3 61.7 reduce-scatter.7
  291.2 60.2 reduce-scatter.5
where the time goes:
time: 407 us; the launch traced here: 405 us
  waiting for transfers between devices  176 us (43%)
  matrix products  79.9 us (20%)
  local copies, waits for them, and re-layouts  55.7 us (14%)
  blocking collectives  40.4 us (10%)
  other arithmetic  37.3 us (9%)
  between operations  14.6 us (4%)
    reduce_scatter x1, waiting for transfers between devices, body(): lax.psum_scatter(dx_part, 'kvh', scatter_dimension=1, tiled=True)  60.5 us
    reduce_scatter x1, waiting for transfers between devices, body(): lax.psum_scatter(second_acc, 'ctx', scatter_dimension=0, tiled=True)  51.5 us
    reduce_scatter x1, waiting for transfers between devices, body(): grad = lax.psum_scatter(dw_part, 'ctx', scatter_dimension=0, tiled=True)  50.2 us
    psum x1, blocking collectives, body(): squares = lax.psum(jnp.sum(grad * grad), ('ctx', 'kvh'))  40.4 us
    unnamed x19, local copies, waits for them, and re-layouts  24.9 us
    dot_general x12, matrix products, block_terms(): jnp.einsum('uyeb,pyb->yeup', output_split[layer_index], value_matrix, pre...  21.1 us
    dynamic_slice x8, local copies, waits for them, and re-layouts, step_block(): kblock = lax.dynamic_slice_in_dim(kv_whole, offset, key_span, 0)  15.7 us
    dot_general x12, matrix products, block_terms(): jnp.einsum('uyeb,pyb->yeup', q_split[layer_index], kmat, preferred_elemen...  15 us
  transfers between devices with their start and end apart: 4, of which 4 were waited for; matrix products, arithmetic and copies ran while one was open for 8% of the time, Pallas kernels for 0%

commit v1 on v0

v1 whole, which is shorter than its diff:
```python
import functools
import math

import jax
import jax.numpy as jnp
from jax import lax
from jax.experimental import pallas as pl
from jax.experimental.pallas import tpu as pltpu
from jax.sharding import PartitionSpec as P

D = 3072
KVH = 8
HD = 128
QBLK = 128
KBLK = 128

NT = (((1,), (1,)), ((), ()))
NN = (((1,), (0,)), ((), ()))
TN = (((0,), (0,)), ((), ()))
F32 = jnp.float32
BF16 = jnp.bfloat16


def dot(a, b, dims):
    return lax.dot_general(a, b, dims, preferred_element_type=F32)


def kernel(
    dims,
    x_ref,
    xs_ref,
    w_ref,
    q_ref,
    o_ref,
    lse_ref,
    delta_ref,
    mask_ref,
    lim_ref,
    dq_ref,
    dx_ref,
    dw_ref,
    kvw,
    xall,
    wall,
    snd,
    rcv,
    dkvc,
    dkvz,
    qt,
    ot,
    dqacc,
    bias,
    acc,
    sqc,
    sqz,
    kv_s,
    kv_r,
    x_s,
    x_r,
    w_s,
    w_r,
    p_s,
    p_r,
    c_s,
    c_r,
    z_s,
    z_r,
    sc_s,
    sc_r,
    sz_s,
    sz_r,
    loc,
):
    C, Z, kvd, G, L, nq, own, total = dims
    me = lax.axis_index("ctx")
    mz = lax.axis_index("kvh")
    cw = xall.shape[2]
    zw = wall.shape[1]
    scale = HD ** (-0.5)
    c2 = scale * math.log2(math.e)
    sliced = cw % 128 == 0
    kper = own // KBLK

    def ctx_copy(src, dst, ss, rs, dev):
        return pltpu.make_async_remote_copy(
            src_ref=src, dst_ref=dst, send_sem=ss, recv_sem=rs,
            device_id={"ctx": dev}, device_id_type=pl.DeviceIdType.MESH)

    def z_copy(src, dst, ss, rs, dev):
        return pltpu.make_async_remote_copy(
            src_ref=src, dst_ref=dst, send_sem=ss, recv_sem=rs,
            device_id={"kvh": dev}, device_id_type=pl.DeviceIdType.MESH)

    def each(n, mine, f, back=False):
        def one(j, carry):
            f(lax.rem(mine + (n - j if back else j), n))
            return carry

        lax.fori_loop(1, n, one, 0)

    def x_cols(d):
        if sliced:
            return x_ref.at[:, pl.ds(pl.multiple_of(d * cw, 128), cw)]
        return xs_ref.at[d]

    def w_rows(d):
        return w_ref.at[pl.ds(pl.multiple_of(d * zw, 128), zw), :]

    def kv_copy(h, d, slot):
        return ctx_copy(kvw.at[h, slot], kvw.at[h, slot], kv_s.at[h, d], kv_r.at[h, slot], d)

    def x_copy(d, slot):
        return ctx_copy(x_cols(d), xall.at[slot], x_s.at[d], x_r.at[slot], d)

    def w_copy(d, slot):
        return z_copy(w_rows(d), wall.at[slot], w_s.at[d], w_r.at[slot], d)

    def p_copy(h, d, slot):
        return ctx_copy(snd.at[h, d], rcv.at[h, slot], p_s.at[h, d], p_r.at[h, slot], d)

    def c_copy(h, d, slot):
        return ctx_copy(dkvc.at[h, slot], dkvc.at[h, slot], c_s.at[h, d], c_r.at[h, slot], d)

    def z_half(h, d, slot):
        return z_copy(dkvz.at[h, slot], dkvz.at[h, slot], z_s.at[h, d], z_r.at[h, slot], d)

    def sc_copy(d, slot):
        return ctx_copy(sqc.at[slot], sqc.at[slot], sc_s.at[d], sc_r.at[slot], d)

    def sz_copy(d, slot):
        return z_copy(sqz.at[slot], sqz.at[slot], sz_s.at[d], sz_r.at[slot], d)

    barrier = pltpu.get_barrier_semaphore()
    each(C, me, lambda d: pl.semaphore_signal(
        barrier, inc=1, device_id={"ctx": d}, device_id_type=pl.DeviceIdType.MESH))
    each(Z, mz, lambda d: pl.semaphore_signal(
        barrier, inc=1, device_id={"kvh": d}, device_id_type=pl.DeviceIdType.MESH))
    own_x = pltpu.make_async_copy(x_cols(me), xall.at[me], loc.at[0])
    own_w = pltpu.make_async_copy(w_rows(mz), wall.at[mz], loc.at[1])
    own_x.start()
    own_w.start()

    for h in range(kvd):
        cols = slice(h * 2 * HD, (h + 1) * 2 * HD)
        kvw[h, me] = dot(x_ref[...], w_ref[:, cols], NN).astype(BF16)
        if h == 0:
            pl.semaphore_wait(barrier, C + Z - 2)
        each(C, me, lambda d: kv_copy(h, d, me).start(), back=True)
    each(Z, mz, lambda d: w_copy(d, mz).start())
    each(C, me, lambda d: x_copy(d, me).start())

    def reduce(h):
        def add(j, total_sum):
            d = lax.rem(me + j, C)
            p_copy(h, d, d).wait_recv()
            return total_sum + rcv[h, d].astype(F32)

        half = lax.fori_loop(1, C, add, snd[h, me].astype(F32)).astype(BF16)
        dkvc[h, me] = half
        dkvz[h, mz] = half
        each(Z, mz, lambda d: z_half(h, d, mz).start())
        each(C, me, lambda d: c_copy(h, d, me).start())

    dqacc[...] = jnp.zeros_like(dqacc)
    for h in range(kvd):

        def turn(l, carry):
            for g in range(G):
                hh = h * G + g
                cols = slice(hh * HD, (hh + 1) * HD)
                qt[l, g] = jnp.transpose(q_ref[l, :, cols])
                ot[l, g] = jnp.transpose(o_ref[l, :, cols])
            return carry

        lax.fori_loop(0, L, turn, 0)
        shift = 1 if (h == kvd - 1 and h > 0) else 0

        def step(s, carry):
            owner = lax.rem(me + s + shift, C)

            @pl.when(owner != me)
            def _():
                kv_copy(h, owner, owner).wait_recv()

            kmat = kvw[h, owner, :, :HD]
            vmat = kvw[h, owner, :, HD:]
            for kb in range(kper):
                rows = mask_ref[owner * kper + kb]
                at = owner * own + kb * KBLK
                pos = at + lax.broadcasted_iota(jnp.int32, (nq, KBLK), 1)
                bias[:, kb * KBLK:(kb + 1) * KBLK] = jnp.where(
                    pos < lim_ref[...], rows, -jnp.inf)
            acc[...] = jnp.zeros_like(acc)

            def layer(l, carry):
                for g in range(G):
                    hh = h * G + g
                    cols = slice(hh * HD, (hh + 1) * HD)
                    q = q_ref[l, :, cols]
                    o = o_ref[l, :, cols]
                    sc = dot(q, kmat, NT)
                    pr = jnp.exp2(sc * c2 - lse_ref[l, :, hh:hh + 1] + bias[...])
                    dp = dot(o, vmat, NT)
                    ds = (pr * (dp - delta_ref[l, :, hh:hh + 1])).astype(BF16)
                    ph = pr.astype(BF16)
                    dqacc[l, hh] += dot(ds, kmat, NN)
                    acc[0] += dot(qt[l, g], ds, NN)
                    acc[1] += dot(ot[l, g], ph, NN)
                return carry

            lax.fori_loop(0, L, layer, 0)
            snd[h, owner, :, :HD] = jnp.transpose(acc[0] * scale).astype(BF16)
            snd[h, owner, :, HD:] = jnp.transpose(acc[1]).astype(BF16)

            @pl.when(owner != me)
            def _():
                p_copy(h, owner, me).start()

            if h > 0:

                @pl.when(s == min(1, C - 1))
                def _():
                    reduce(h - 1)

            return carry

        lax.fori_loop(0, C, step, 0)

    reduce(kvd - 1)

    def finish(l, carry):
        for hh in range(kvd * G):
            dq_ref[l, :, hh * HD:(hh + 1) * HD] = (dqacc[l, hh] * scale).astype(BF16)
        return carry

    lax.fori_loop(0, L, finish, 0)
    own_x.wait()
    own_w.wait()
    each(C, me, lambda d: x_copy(d, d).wait_recv())
    each(Z, mz, lambda d: w_copy(d, d).wait_recv())

    for h in range(kvd):
        cols = slice(h * 2 * HD, (h + 1) * 2 * HD)

        def grad(j, tot):
            d = lax.rem(me + j, C)

            @pl.when(j > 0)
            def _():
                c_copy(h, d, d).wait_recv()

            return tot + dot(xall[d], dkvc[h, d], TN)

        dw_ref[:, cols] = lax.fori_loop(0, C, grad, jnp.zeros((cw, 2 * HD), F32))
    g = dw_ref[...]
    sqc[me] = jnp.broadcast_to(jnp.sum(g * g, axis=(0, 1), keepdims=True), sqc.shape[1:])
    each(C, me, lambda d: sc_copy(d, me).start())

    dx = jnp.zeros(dx_ref.shape, F32)
    for h in range(kvd):
        cols = slice(h * 2 * HD, (h + 1) * 2 * HD)

        def part(j, tot):
            d = lax.rem(mz + j, Z)

            @pl.when(j > 0)
            def _():
                z_half(h, d, d).wait_recv()

            return tot + dot(dkvz[h, d], wall[d, :, cols], NT)

        dx = lax.fori_loop(0, Z, part, dx)
        if h == 0:
            each(C, me, lambda d: sc_copy(d, d).wait_recv())
            sqz[mz] = jnp.sum(sqc[...], axis=0)
            each(Z, mz, lambda d: sz_copy(d, mz).start())
    dx_ref[...] = dx.astype(BF16)

    each(Z, mz, lambda d: sz_copy(d, d).wait_recv())
    msq = jnp.sum(sqz[...], axis=0)[:1, :1] / total
    inv = 1.0 / jnp.sqrt(msq + 1e-6)
    dw_ref[...] = dw_ref[...] * inv

    def drain_ctx(d):
        for h in range(kvd):
            kv_copy(h, d, me).wait_send()
            p_copy(h, d, me).wait_send()
            c_copy(h, d, me).wait_send()
        x_copy(d, me).wait_send()
        sc_copy(d, me).wait_send()

    def drain_z(d):
        for h in range(kvd):
            z_half(h, d, mz).wait_send()
        w_copy(d, mz).wait_send()
        sz_copy(d, mz).wait_send()

    each(C, me, drain_ctx)
    each(Z, mz, drain_z)


def body(x_kv, w_kv, queries, d_out, lse, delta, offsets, block_mask):
    L, nq, width = queries.shape
    C, Z = lax.axis_size("ctx"), lax.axis_size("kvh")
    own, dm = x_kv.shape
    kvd = w_kv.shape[1] // (2 * HD)
    heads = width // HD
    G = heads // kvd
    cw, zw = dm // C, dm // Z
    qblocks, kblocks = block_mask.shape
    rows = jnp.transpose(jnp.where(block_mask == 1, 0.0, -jnp.inf).astype(F32))
    mask = jnp.broadcast_to(rows[:, :, None, None], (kblocks, qblocks, nq // qblocks, 1))
    mask = mask.reshape(kblocks, nq, 1)
    lim = (offsets[0] + jnp.arange(nq, dtype=jnp.int32))[:, None]
    if cw % 128 == 0:
        xs = jnp.zeros((8, 128), BF16)
    else:
        xs = jnp.transpose(x_kv.reshape(own, C, cw), (1, 0, 2))
    total = float(dm) * Z * kvd * 2 * HD
    dims = (C, Z, kvd, G, L, nq, own, total)
    vm = pl.BlockSpec(memory_space=pltpu.VMEM)
    blk = (own, 2 * HD)
    dma = pltpu.SemaphoreType.DMA
    flops = 2 * L * heads * nq * own * C * HD * 5
    return pl.pallas_call(
        functools.partial(kernel, dims),
        out_shape=(
            jax.ShapeDtypeStruct(queries.shape, BF16),
            jax.ShapeDtypeStruct((own, zw), BF16),
            jax.ShapeDtypeStruct((cw, kvd * 2 * HD), F32),
        ),
        in_specs=[vm] * 9,
        out_specs=(vm, vm, vm),
        scratch_shapes=[
            pltpu.VMEM((kvd, C) + blk, BF16),
            pltpu.VMEM((C, own, cw), BF16),
            pltpu.VMEM((Z, zw, kvd * 2 * HD), BF16),
            pltpu.VMEM((kvd, C) + blk, BF16),
            pltpu.VMEM((kvd, C) + blk, BF16),
            pltpu.VMEM((kvd, C) + blk, BF16),
            pltpu.VMEM((kvd, Z) + blk, BF16),
            pltpu.VMEM((L, G, HD, nq), BF16),
            pltpu.VMEM((L, G, HD, nq), BF16),
            pltpu.VMEM((L, heads, nq, HD), F32),
            pltpu.VMEM((nq, own), F32),
            pltpu.VMEM((2, HD, own), F32),
            pltpu.VMEM((C, 8, 128), F32),
            pltpu.VMEM((Z, 8, 128), F32),
            dma((kvd, C)), dma((kvd, C)),
            dma((C,)), dma((C,)),
            dma((Z,)), dma((Z,)),
            dma((kvd, C)), dma((kvd, C)),
            dma((kvd, C)), dma((kvd, C)),
            dma((kvd, Z)), dma((kvd, Z)),
            dma((C,)), dma((C,)),
            dma((Z,)), dma((Z,)),
            dma((2,)),
        ],
        compiler_params=pltpu.CompilerParams(
            collective_id=0, has_side_effects=True, vmem_limit_bytes=60 * 1024 * 1024
        ),
        cost_estimate=pl.CostEstimate(flops=flops, bytes_accessed=1 << 24, transcendentals=0),
    )(x_kv, xs, w_kv, queries, d_out, lse * math.log2(math.e), delta, mask, lim)


def solution(mesh):
    in_specs = (
        P("ctx", None),
        P(None, "kvh"),
        P(None, "ctx", "kvh"),
        P(None, "ctx", "kvh"),
        P(None, "ctx", "kvh"),
        P(None, "ctx", "kvh"),
        P("ctx"),
        P("ctx", None),
    )
    out_specs = (P(None, "ctx", "kvh"), P("ctx", "kvh"), P("ctx", "kvh"))
    return jax.shard_map(body, mesh=mesh, in_specs=in_specs, out_specs=out_specs, check_vma=False)
```

time: 407 us -> 128 us (0.31)
  waiting for transfers between devices: 176 us -> 0 us
  Pallas kernels: 0 us -> 112 us
  matrix products: 79.9 us -> 0 us
  local copies, waits for them, and re-layouts: 55.7 us -> 12.1 us
  blocking collectives: 40.4 us -> 0 us
  other arithmetic: 37.3 us -> 2.26 us
  between operations: 14.6 us -> 1.33 us
    reduce_scatter x3 -> x0, waiting for transfers between devices: 162 us -> none  [the longest x1 60.5 us: body(): lax.psum_scatter(dx_part, 'kvh', scatter_dimension=1, tiled=True)]
    pallas_call x0 -> x1, Pallas kernels: none -> 112 us  [body(): pl.pallas_call(functools.partial(kernel, dims), out_shape=(jax.ShapeDtype...]
    dot_general x63 -> x0, matrix products: 79.9 us -> none  [the longest x12 21.1 us: block_terms(): jnp.einsum('uyeb,pyb->yeup', output_split[layer_index], value_matrix, pre...]
    psum x1 -> x0, blocking collectives: 40.4 us -> none  [body(): squares = lax.psum(jnp.sum(grad * grad), ('ctx', 'kvh'))]
    dynamic_slice x16 -> x0, local copies, waits for them, and re-layouts: 20.8 us -> none  [the longest x8 15.7 us: step_block(): kblock = lax.dynamic_slice_in_dim(kv_whole, offset, key_span, 0)]
    unnamed x19 -> x11, local copies, waits for them, and re-layouts: 24.9 us -> 6.61 us
    all_gather x1 -> x0, waiting for transfers between devices: 13.6 us -> none  [body(): kv_whole = lax.all_gather(kv_local, 'ctx', axis=0, tiled=True)]
    dynamic_update_slice x4 -> x0, other arithmetic: 12.8 us -> none  [one_block(): lax.dynamic_update_slice_in_dim(second, current + dkv_part, at, 0)]
  transfers between devices with their start and end apart: 4 -> 0, of which waited for: 4 -> 0; matrix products, arithmetic and copies ran while one was open for 8% -> 0% of each run, Pallas kernels for 0% -> 0%
where the time goes in v1:
time: 128 us
  Pallas kernels  112 us (88%)
  local copies, waits for them, and re-layouts  12.1 us (9%)
  other arithmetic  2.26 us (2%)
  between operations  1.33 us (1%)
    pallas_call x1, Pallas kernels, body(): pl.pallas_call(functools.partial(kernel, dims), out_shape=(jax.ShapeDtype...  112 us
    unnamed x11, local copies, waits for them, and re-layouts  6.61 us
    broadcast_in_dim x2, local copies, waits for them, and re-layouts, body(): jnp.broadcast_to(rows[:, :, None, None], (kblocks, qblocks, nq // qblocks...  4.85 us

profile of v1, /device:TPU:0, one launch (start us, length us, event | category | flops | bytes accessed | tf_op | source)
XLA Modules:
  0.0 127.5 jit_solution(17746591098137344506)
XLA Ops:
  0.6 0.0 copy-start.2
  1.3 0.7 select_bitcast_fusion
  2.0 0.1 copy.20
  2.1 0.1 broadcast_in_dim.23
  2.1 0.7 iota_add_fusion.lim_ref
  2.8 1.0 copy.18
  3.9 0.9 broadcast_multiply_fusion.lse_ref
  4.7 0.0 copy-done.2
  4.7 1.1 copy.21.delta_ref
  5.8 4.8 %broadcast_in_dim.25.mask_ref = f32[16,384,1]{2,1,0:T(8,128)} reshape(f32[16,3,128]{2,1,0:T(4,128)S(1)} %broadcast_in_dim.23) | data formatting | bytes 49152 | tf_op jit(solution)/shard_map/broadcast_in_dim | solution.py:312
  10.6 0.6 broadcast_in_dim.20.xs_ref
  11.2 111.8 %shard_map.103 = (bf16[3,384,768]{2,1,0:T(8,128)(2,1)}, bf16[256,768]{1,0:T(8,128)(2,1)}, f32[384,512]{1,0:T(8,128)}) custom-call(bf16[256,3072]{1,0:T(8,128)(2,1)} %x_ref.1, bf16[8,128]{1,0:T(8,128)(2,1)} %broadcast_in_dim.20.xs_ref, bf16[3072,512]{1,0:T(8,128)(2,1)} %w_ref.1, bf16[3,384,768]{2,1,0:T(8,128)(2,1)} %q_ref.1, bf16[3,384,768]{2,1,0:T(8,128)(2,1)} %o_ref.1, ...), custom_call_target="tpu_custom_call" | custom-call | flops 18119393280 | bytes 16777216 | tf_op jit(solution)/shard_map/pallas_call | solution.py:325
  123.0 0.0 copy-start.1
  123.0 0.0 copy-start
  123.0 2.9 %copy.27 = bf16[3,384,768]{2,1,0:T(8,128)(2,1)} copy(bf16[3,384,768]{2,1,0:T(8,128)(2,1)} %get-tuple-element.6) | data formatting | bytes 3538944
  125.9 0.0 copy-done.1
  125.9 0.7 copy.28
  126.6 0.0 copy-done
  126.6 0.9 copy.29
Async XLA Ops:
  0.6 4.1 %copy-start.2 = (f32[3,384,6]{1,2,0:T(8,128)S(1)}, f32[3,384,6]{1,2,0:T(8,128)}, u32[]{:S(2)}) copy-start(f32[3,384,6]{1,2,0:T(8,128)} %param.13) | copy-start | bytes 82948
  123.0 2.9 %copy-start.1 = (bf16[256,768]{1,0:T(8,128)(2,1)S(1)}, bf16[256,768]{1,0:T(8,128)(2,1)}, u32[]{:S(2)}) copy-start(bf16[256,768]{1,0:T(8,128)(2,1)} %get-tuple-element.7) | copy-start | bytes 1179652
  123.0 3.7 %copy-start = (f32[384,512]{1,0:T(8,128)S(1)}, f32[384,512]{1,0:T(8,128)}, u32[]{:S(2)}) copy-start(f32[384,512]{1,0:T(8,128)} %get-tuple-element.8) | copy-start | bytes 2359300

commit v2 on v1

v2 whole, which is shorter than its diff:
```python
import functools
import math

import jax
import jax.numpy as jnp
from jax import lax
from jax.experimental import pallas as pl
from jax.experimental.pallas import tpu as pltpu
from jax.sharding import PartitionSpec as P

D = 3072
KVH = 8
HD = 128
QBLK = 128
KBLK = 128

NT = (((1,), (1,)), ((), ()))
NN = (((1,), (0,)), ((), ()))
TN = (((0,), (0,)), ((), ()))
F32 = jnp.float32
BF16 = jnp.bfloat16


def dot(a, b, dims):
    return lax.dot_general(a, b, dims, preferred_element_type=F32)


def kernel(
    dims,
    x_ref,
    xs_ref,
    w_ref,
    q_ref,
    o_ref,
    lse_ref,
    delta_ref,
    mask_ref,
    off_ref,
    dq_ref,
    dx_ref,
    dw_ref,
    kvw,
    xall,
    wall,
    snd,
    prt,
    rcv,
    dkvc,
    dkvz,
    qt,
    ot,
    lse2,
    dqacc,
    bias,
    acc,
    sqc,
    sqz,
    kv_s,
    kv_f,
    kv_r,
    x_s,
    x_r,
    w_s,
    w_r,
    wf_s,
    wf_r,
    pp_s,
    pp_r,
    p_s,
    p_r,
    c_s,
    c_f,
    c_r,
    z_s,
    z_r,
    sc_s,
    sc_r,
    sz_s,
    sz_r,
    loc,
):
    C, Z, kvd, G, L, nq, own, total = dims
    me = lax.axis_index("ctx")
    mz = lax.axis_index("kvh")
    cw = xall.shape[2]
    zw = wall.shape[2] * 2
    chips = C // 2
    chip, core = me // 2, lax.rem(me, 2)
    mate = chip * 2 + 1 - core
    hw = zw // 2
    scale = HD ** (-0.5)
    c2 = scale * math.log2(math.e)
    sliced = cw % 128 == 0
    kper = own // KBLK

    def ctx_copy(src, dst, ss, rs, dev):
        return pltpu.make_async_remote_copy(
            src_ref=src, dst_ref=dst, send_sem=ss, recv_sem=rs,
            device_id={"ctx": dev}, device_id_type=pl.DeviceIdType.MESH)

    def z_copy(src, dst, ss, rs, dev):
        return pltpu.make_async_remote_copy(
            src_ref=src, dst_ref=dst, send_sem=ss, recv_sem=rs,
            device_id={"kvh": dev}, device_id_type=pl.DeviceIdType.MESH)

    def each(n, mine, f, back=False):
        def one(j, carry):
            f(lax.rem(mine + (n - j if back else j), n))
            return carry

        lax.fori_loop(1, n, one, 0)

    def x_cols(d):
        if sliced:
            return x_ref.at[:, pl.ds(pl.multiple_of(d * cw, 128), cw)]
        return xs_ref.at[d]

    def w_rows(d):
        return w_ref.at[pl.ds(pl.multiple_of(d * zw + core * hw, 64), hw), :]

    def same_core(t):
        return t * 2 + core

    def kv_copy(h, d):
        return ctx_copy(kvw.at[h, me], kvw.at[h, me], kv_s.at[h, d], kv_r.at[h, me], d)

    def kv_pass(h, t):
        k = same_core(t)
        return ctx_copy(kvw.at[h, k], kvw.at[h, k], kv_f.at[h, t], kv_r.at[h, k], mate)

    def kv_wait(h, k):
        ctx_copy(kvw.at[h, k], kvw.at[h, k], kv_s.at[h, k], kv_r.at[h, k], mate).wait_recv()

    def x_copy(d, slot):
        return ctx_copy(x_cols(d), xall.at[slot], x_s.at[d], x_r.at[slot], d)

    def w_copy(d, slot):
        return z_copy(w_rows(d), wall.at[slot, core], w_s.at[d], w_r.at[slot], d)

    def w_pass(d, part):
        return ctx_copy(wall.at[d, part], wall.at[d, part], wf_s.at[d], wf_r.at[d], mate)

    def pp_copy(h, t):
        return ctx_copy(snd.at[h, t * 2 + 1 - core], prt.at[h, t], pp_s.at[h, t], pp_r.at[h, t], mate)

    def p_copy(h, t, slot):
        return ctx_copy(
            snd.at[h, same_core(t)], rcv.at[h, slot], p_s.at[h, t], p_r.at[h, slot], same_core(t))

    def c_copy(h, d):
        return ctx_copy(dkvc.at[h, me], dkvc.at[h, me], c_s.at[h, d], c_r.at[h, me], d)

    def c_pass(h, t):
        k = same_core(t)
        return ctx_copy(dkvc.at[h, k], dkvc.at[h, k], c_f.at[h, t], c_r.at[h, k], mate)

    def c_wait(h, k):
        ctx_copy(dkvc.at[h, k], dkvc.at[h, k], c_s.at[h, k], c_r.at[h, k], mate).wait_recv()

    def z_half(h, d, slot):
        return z_copy(dkvz.at[h, slot], dkvz.at[h, slot], z_s.at[h, d], z_r.at[h, slot], d)

    def sc_copy(d, slot):
        return ctx_copy(sqc.at[slot], sqc.at[slot], sc_s.at[d], sc_r.at[slot], d)

    def sz_copy(d, slot):
        return z_copy(sqz.at[slot], sqz.at[slot], sz_s.at[d], sz_r.at[slot], d)

    barrier = pltpu.get_barrier_semaphore()
    each(C, me, lambda d: pl.semaphore_signal(
        barrier, inc=1, device_id={"ctx": d}, device_id_type=pl.DeviceIdType.MESH))
    each(Z, mz, lambda d: pl.semaphore_signal(
        barrier, inc=1, device_id={"kvh": d}, device_id_type=pl.DeviceIdType.MESH))
    own_x = pltpu.make_async_copy(x_cols(me), xall.at[me], loc.at[0])
    own_w = pltpu.make_async_copy(w_rows(mz), wall.at[mz, core], loc.at[1])
    own_x.start()
    own_w.start()

    for h in range(kvd):
        cols = slice(h * 2 * HD, (h + 1) * 2 * HD)
        kvw[h, me] = dot(x_ref[...], w_ref[:, cols], NN).astype(BF16)
        if h == 0:
            pl.semaphore_wait(barrier, C + Z - 2)
        kv_copy(h, mate).start()
        each(chips, chip, lambda t: kv_copy(h, same_core(t)).start(), back=True)
    each(Z, mz, lambda d: w_copy(d, mz).start())
    lse2[...] = lse_ref[...] * math.log2(math.e)

    def reduce(h):
        def add(j, total_sum):
            t = lax.rem(chip + j, chips)
            p_copy(h, t, t).wait_recv()
            return total_sum + rcv[h, t].astype(F32)

        half = lax.fori_loop(1, chips, add, snd[h, me].astype(F32)).astype(BF16)
        dkvc[h, me] = half
        dkvz[h, mz] = half
        each(Z, mz, lambda d: z_half(h, d, mz).start())
        c_copy(h, mate).start()
        each(chips, chip, lambda t: c_copy(h, same_core(t)).start())

    dqacc[...] = jnp.zeros_like(dqacc)
    for h in range(kvd):

        def turn(l, carry):
            for g in range(G):
                hh = h * G + g
                cols = slice(hh * HD, (hh + 1) * HD)
                qt[l, g] = jnp.transpose(q_ref[l, :, cols])
                ot[l, g] = jnp.transpose(o_ref[l, :, cols])
            return carry

        lax.fori_loop(0, L, turn, 0)
        shift = 1 if (h == kvd - 1 and h > 0) else 0

        def step(s, carry):
            t = lax.rem(chip + s // 2 + shift, chips)
            first = lax.rem(s, 2) == 0
            owner = t * 2 + jnp.where(first, 1 - core, core)

            if shift:

                @pl.when(s == 0)
                def _():
                    kv_wait(h, same_core(t))
                    kv_pass(h, t).start()

            @pl.when(first)
            def _():
                kv_wait(h, owner)

            after = lax.rem(t + 1, chips)

            @pl.when(jnp.logical_not(first) & (after != chip) & (s < C - 1))
            def _():
                kv_wait(h, same_core(after))
                kv_pass(h, after).start()

            kmat = kvw[h, owner, :, :HD]
            vmat = kvw[h, owner, :, HD:]
            for kb in range(kper):
                at = owner * own + kb * KBLK
                gap = at + lax.broadcasted_iota(jnp.int32, (QBLK, KBLK), 1)
                gap = gap - lax.broadcasted_iota(jnp.int32, (QBLK, KBLK), 0)
                for qb in range(nq // QBLK):
                    open_block = mask_ref[qb, owner * kper + kb] == 1
                    limit = jnp.where(open_block, off_ref[0] + qb * QBLK, -(1 << 30))
                    bias[qb * QBLK:(qb + 1) * QBLK, kb * KBLK:(kb + 1) * KBLK] = jnp.where(
                        gap < limit, 0.0, -jnp.inf)
            acc[...] = jnp.zeros_like(acc)

            def layer(l, carry):
                for g in range(G):
                    hh = h * G + g
                    cols = slice(hh * HD, (hh + 1) * HD)
                    q = q_ref[l, :, cols]
                    o = o_ref[l, :, cols]
                    sc = dot(q, kmat, NT)
                    pr = jnp.exp2(sc * c2 - lse2[l, :, hh:hh + 1] + bias[...])
                    dp = dot(o, vmat, NT)
                    ds = (pr * (dp - delta_ref[l, :, hh:hh + 1])).astype(BF16)
                    ph = pr.astype(BF16)
                    dqacc[l, hh] += dot(ds, kmat, NN)
                    acc[0] += dot(qt[l, g], ds, NN)
                    acc[1] += dot(ot[l, g], ph, NN)
                return carry

            for l in range(L):
                layer(l, 0)
            snd[h, owner, :, :HD] = jnp.transpose(acc[0] * scale).astype(BF16)
            snd[h, owner, :, HD:] = jnp.transpose(acc[1]).astype(BF16)

            @pl.when(first)
            def _():
                pp_copy(h, t).start()

            @pl.when(jnp.logical_not(first))
            def _():
                pp_copy(h, t).wait_recv()
                both = snd[h, owner].astype(F32) + prt[h, t].astype(F32)
                snd[h, owner] = both.astype(BF16)

                @pl.when(t != chip)
                def _():
                    p_copy(h, t, chip).start()

            if h == 0:

                @pl.when(s == min(2, C - 1))
                def _():
                    each(C, me, lambda d: x_copy(d, me).start())

            if h == kvd - 1:

                @pl.when(s == C - 1)
                def _():
                    own_w.wait()
                    w_pass(mz, core).start()

                    def pass_on(d):
                        w_copy(d, d).wait_recv()
                        w_pass(d, core).start()

                    each(Z, mz, pass_on)

            if h > 0:

                @pl.when(s == min(1, C - 1))
                def _():
                    reduce(h - 1)

            return carry

        lax.fori_loop(0, C, step, 0)

    reduce(kvd - 1)

    def finish(l, carry):
        for hh in range(kvd * G):
            dq_ref[l, :, hh * HD:(hh + 1) * HD] = (dqacc[l, hh] * scale).astype(BF16)
        return carry

    lax.fori_loop(0, L, finish, 0)
    own_x.wait()
    each(C, me, lambda d: x_copy(d, d).wait_recv())

    for h in range(kvd):

        def gather(j, carry):
            t = lax.rem(chip + j, chips)
            c_wait(h, same_core(t))
            c_pass(h, t).start()
            return carry

        lax.fori_loop(1, chips, gather, 0)
    for h in range(kvd):
        each(chips, chip, lambda t: c_wait(h, t * 2 + 1 - core))
        c_wait(h, mate)
    x_all = xall[...].reshape(C * own, cw)
    dkv_all = jnp.concatenate([dkvc[h].reshape(C * own, 2 * HD) for h in range(kvd)], axis=1)
    dw_ref[...] = dot(x_all, dkv_all, TN)
    g = dw_ref[...]
    sqc[me] = jnp.broadcast_to(jnp.sum(g * g, axis=(0, 1), keepdims=True), sqc.shape[1:])
    each(C, me, lambda d: sc_copy(d, me).start())

    w_pass(mz, 1 - core).wait_recv()
    each(Z, mz, lambda d: w_pass(d, 1 - core).wait_recv())
    each(C, me, lambda d: sc_copy(d, d).wait_recv())
    sqz[mz] = jnp.sum(sqc[...], axis=0)
    each(Z, mz, lambda d: sz_copy(d, mz).start())
    for h in range(kvd):
        each(Z, mz, lambda d: z_half(h, d, d).wait_recv())
    dkv_z = jnp.concatenate([dkvz[h, d] for d in range(Z) for h in range(kvd)], axis=1)
    dx = []
    for k in range(2):
        w_all = jnp.concatenate([wall[d, k] for d in range(Z)], axis=1)
        dx.append(dot(dkv_z, w_all, NT))
    dx_ref[...] = jnp.concatenate(dx, axis=1).astype(BF16)

    each(Z, mz, lambda d: sz_copy(d, d).wait_recv())
    msq = jnp.sum(sqz[...], axis=0)[:1, :1] / total
    inv = 1.0 / jnp.sqrt(msq + 1e-6)
    dw_ref[...] = dw_ref[...] * inv

    def drain_chip(t):
        for h in range(kvd):
            kv_copy(h, same_core(t)).wait_send()
            kv_pass(h, t).wait_send()
            p_copy(h, t, chip).wait_send()
            pp_copy(h, t).wait_send()
            c_copy(h, same_core(t)).wait_send()
            c_pass(h, t).wait_send()

    def drain_ctx(d):
        x_copy(d, me).wait_send()
        sc_copy(d, me).wait_send()

    def drain_z(d):
        for h in range(kvd):
            z_half(h, d, mz).wait_send()
        w_copy(d, mz).wait_send()
        w_pass(d, core).wait_send()
        sz_copy(d, mz).wait_send()

    for h in range(kvd):
        kv_copy(h, mate).wait_send()
        pp_copy(h, chip).wait_send()
        c_copy(h, mate).wait_send()
    w_pass(mz, core).wait_send()
    each(chips, chip, drain_chip)
    each(C, me, drain_ctx)
    each(Z, mz, drain_z)


def body(x_kv, w_kv, queries, d_out, lse, delta, offsets, block_mask):
    L, nq, width = queries.shape
    C, Z = lax.axis_size("ctx"), lax.axis_size("kvh")
    own, dm = x_kv.shape
    kvd = w_kv.shape[1] // (2 * HD)
    heads = width // HD
    G = heads // kvd
    cw, zw = dm // C, dm // Z
    if cw % 128 == 0:
        xs = jnp.zeros((8, 128), BF16)
    else:
        xs = jnp.transpose(x_kv.reshape(own, C, cw), (1, 0, 2))
    total = float(dm) * Z * kvd * 2 * HD
    dims = (C, Z, kvd, G, L, nq, own, total)
    vm = pl.BlockSpec(memory_space=pltpu.VMEM)
    blk = (own, 2 * HD)
    dma = pltpu.SemaphoreType.DMA
    flops = 2 * L * heads * nq * own * C * HD * 5
    return pl.pallas_call(
        functools.partial(kernel, dims),
        out_shape=(
            jax.ShapeDtypeStruct(queries.shape, BF16),
            jax.ShapeDtypeStruct((own, zw), BF16),
            jax.ShapeDtypeStruct((cw, kvd * 2 * HD), F32),
        ),
        in_specs=[vm] * 7 + [pl.BlockSpec(memory_space=pltpu.SMEM)] * 2,
        out_specs=(vm, vm, vm),
        scratch_shapes=[
            pltpu.VMEM((kvd, C) + blk, BF16),
            pltpu.VMEM((C, own, cw), BF16),
            pltpu.VMEM((Z, 2, zw // 2, kvd * 2 * HD), BF16),
            pltpu.VMEM((kvd, C) + blk, BF16),
            pltpu.VMEM((kvd, C // 2) + blk, BF16),
            pltpu.VMEM((kvd, C // 2) + blk, BF16),
            pltpu.VMEM((kvd, C) + blk, BF16),
            pltpu.VMEM((kvd, Z) + blk, BF16),
            pltpu.VMEM((L, G, HD, nq), BF16),
            pltpu.VMEM((L, G, HD, nq), BF16),
            pltpu.VMEM(lse.shape, F32),
            pltpu.VMEM((L, heads, nq, HD), F32),
            pltpu.VMEM((nq, own), F32),
            pltpu.VMEM((2, HD, own), F32),
            pltpu.VMEM((C, 8, 128), F32),
            pltpu.VMEM((Z, 8, 128), F32),
            dma((kvd, C)), dma((kvd, C // 2)), dma((kvd, C)),
            dma((C,)), dma((C,)),
            dma((Z,)), dma((Z,)),
            dma((Z,)), dma((Z,)),
            dma((kvd, C // 2)), dma((kvd, C // 2)),
            dma((kvd, C // 2)), dma((kvd, C // 2)),
            dma((kvd, C)), dma((kvd, C // 2)), dma((kvd, C)),
            dma((kvd, Z)), dma((kvd, Z)),
            dma((C,)), dma((C,)),
            dma((Z,)), dma((Z,)),
            dma((2,)),
        ],
        compiler_params=pltpu.CompilerParams(
            collective_id=0, has_side_effects=True, vmem_limit_bytes=60 * 1024 * 1024
        ),
        cost_estimate=pl.CostEstimate(flops=flops, bytes_accessed=1 << 24, transcendentals=0),
    )(x_kv, xs, w_kv, queries, d_out, lse, delta, block_mask, offsets)


def solution(mesh):
    in_specs = (
        P("ctx", None),
        P(None, "kvh"),
        P(None, "ctx", "kvh"),
        P(None, "ctx", "kvh"),
        P(None, "ctx", "kvh"),
        P(None, "ctx", "kvh"),
        P("ctx"),
        P("ctx", None),
    )
    out_specs = (P(None, "ctx", "kvh"), P("ctx", "kvh"), P("ctx", "kvh"))
    return jax.shard_map(body, mesh=mesh, in_specs=in_specs, out_specs=out_specs, check_vma=False)
```

time: 128 us -> 94.4 us (0.74)
  Pallas kernels: 112 us -> 84.1 us
  local copies, waits for them, and re-layouts: 12.1 us -> 8.77 us
  other arithmetic: 2.26 us -> 0 us
    pallas_call x1, Pallas kernels: 112 us -> 84.1 us  [body(): pl.pallas_call(functools.partial(kernel, dims), out_shape=(jax.ShapeDtype...]
    broadcast_in_dim x2 -> x0, local copies, waits for them, and re-layouts: 4.85 us -> none  [body(): jnp.broadcast_to(rows[:, :, None, None], (kblocks, qblocks, nq // qblocks...]
    unnamed x11 -> x9, local copies, waits for them, and re-layouts: 6.61 us -> 8.19 us
where the time goes in v2:
time: 94.4 us; the launch traced here: 94.2 us
  Pallas kernels  84.1 us (89%)
  local copies, waits for them, and re-layouts  8.77 us (9%)
  between operations  1.3 us (1%)
    pallas_call x1, Pallas kernels, body(): pl.pallas_call(functools.partial(kernel, dims), out_shape=(jax.ShapeDtype...  84.1 us
    unnamed x9, local copies, waits for them, and re-layouts  8.19 us

profile of v2, /device:TPU:0, one launch (start us, length us, event | category | flops | bytes accessed | tf_op | source)
XLA Modules:
  0.0 94.2 jit_solution(13825408415848007401)
XLA Ops:
  1.3 1.8 %copy.11.lse_ref = f32[3,384,6]{2,1,0:T(8,128)} copy(f32[3,384,6]{1,2,0:T(8,128)} %param.12) | data formatting | bytes 55296 | tf_op args[4]
  3.1 1.8 %copy.12.delta_ref = f32[3,384,6]{2,1,0:T(8,128)} copy(f32[3,384,6]{1,2,0:T(8,128)} %param.13) | data formatting | bytes 55296 | tf_op args[5]
  4.9 0.6 broadcast_in_dim.3.xs_ref
  5.5 84.1 %shard_map.103 = (bf16[3,384,768]{2,1,0:T(8,128)(2,1)}, bf16[256,768]{1,0:T(8,128)(2,1)}, f32[384,512]{1,0:T(8,128)}) custom-call(bf16[256,3072]{1,0:T(8,128)(2,1)} %x_ref.1, bf16[8,128]{1,0:T(8,128)(2,1)} %broadcast_in_dim.3.xs_ref, bf16[3072,512]{1,0:T(8,128)(2,1)} %w_ref.1, bf16[3,384,768]{2,1,0:T(8,128)(2,1)} %q_ref.1, bf16[3,384,768]{2,1,0:T(8,128)(2,1)} %o_ref.1, ...), custom_call_target="tpu_custom_call" | custom-call | flops 18119393280 | bytes 16777216 | tf_op jit(solution)/shard_map/pallas_call | solution.py:413
  89.6 0.0 copy-start.1
  89.6 0.0 copy-start
  89.6 2.9 %copy.17 = bf16[3,384,768]{2,1,0:T(8,128)(2,1)} copy(bf16[3,384,768]{2,1,0:T(8,128)(2,1)} %get-tuple-element.6) | data formatting | bytes 3538944
  92.5 0.0 copy-done.1
  92.5 0.7 copy.18
  93.3 0.0 copy-done
  93.3 0.9 copy.19
Async XLA Ops:
  89.6 2.9 %copy-start.1 = (bf16[256,768]{1,0:T(8,128)(2,1)S(1)}, bf16[256,768]{1,0:T(8,128)(2,1)}, u32[]{:S(2)}) copy-start(bf16[256,768]{1,0:T(8,128)(2,1)} %get-tuple-element.7) | copy-start | bytes 1179652
  89.6 3.7 %copy-start = (f32[384,512]{1,0:T(8,128)S(1)}, f32[384,512]{1,0:T(8,128)}, u32[]{:S(2)}) copy-start(f32[384,512]{1,0:T(8,128)} %get-tuple-element.8) | copy-start | bytes 2359300
